TPU v7x, 256 devices: a whole 4x4x8 slice. The times are simulated.
256 devices in a mesh: tensor: 8 (over x, core), dp: 32 (over y, z).
Axes of the slice: x: 4, y: 4, z: 8, core: 2. Of those that a mesh axis runs over, the one named last changes fastest.
Arguments:
- tokens: bfloat16 [32768, 6144], P(('dp', 'tensor')), may hold values from -24 to 24
- sample_id: int32 [32, 1024], P('dp'), may hold values from 0 to 7, never falling along the last dimension, each value on 1 to 256 neighbouring positions
- timestep: int32 [32, 8], P('dp'), may hold values from 0 to 31
- step_table: float32 [32, 2, 6144], replicated, may hold values from -3 to 3
- weight: bfloat16 [6144, 3072], P(None, 'tensor'), may hold values from -0.078125 to 0.078125
- grad_q: bfloat16 [32768, 3072], P('dp', 'tensor'), may hold values from -6 to 6
Outputs:
- grad_x: bfloat16 [32768, 6144], P(('dp', 'tensor'))
- grad_weight: float32 [6144, 3072], P('dp', 'tensor')
- grad_table: float32 [32, 2, 6144], replicated
Inputs may be any that keep to these rules, and one draw needn't show every extreme that they name: `sample_id`: within each replica the ids never fall along its rows, and each of the 8 samples has rows.
All inputs are finite; a program needn't handle non-finite values.
Results may differ from a plain program's by a relative error of at most 0.02.
Values may be sent and summed in bfloat16 or wider, within the bound.
A program may use at most 192 MiB of HBM per device.

v0:
```python
import jax
import jax.numpy as jnp
from jax import lax
from jax.sharding import PartitionSpec as P


def normalize(rows_in):
    widened = rows_in.astype(jnp.float32)
    row_mean = jnp.mean(widened, axis=-1, keepdims=True)
    centred = widened - row_mean
    variance = jnp.mean(centred * centred, axis=-1, keepdims=True)
    inv_std = lax.rsqrt(variance + 1e-06)
    return (centred * inv_std, inv_std)


def row_steps(block_ids, step_of_sample, step_count):
    samples = step_of_sample.shape[0]
    sample_hot = (block_ids[:, None] == jnp.arange(samples, dtype=jnp.int32)[None, :]).astype(
        jnp.int32
    )
    step_of_row = jnp.sum(sample_hot * step_of_sample[None, :], axis=1)
    return (step_of_row[:, None] == jnp.arange(step_count, dtype=jnp.int32)[None, :]).astype(
        jnp.float32
    )


def modulation(hot_rows, step_table):
    feature_count = step_table.shape[2]
    table_flat = step_table.reshape(step_table.shape[0], 2 * feature_count)
    modulation_rows = jnp.dot(hot_rows, table_flat, precision=lax.Precision.HIGHEST)
    return (modulation_rows[:, :feature_count], modulation_rows[:, feature_count:])


def body(tokens, sample_id, timestep, step_table, weight, grad_q):
    row_count = tokens.shape[0]
    ids_all = sample_id[0]
    step_of_sample = timestep[0]
    step_count = step_table.shape[0]
    own_ids = lax.dynamic_slice_in_dim(ids_all, lax.axis_index("tensor") * row_count, row_count, 0)
    normed, inv_std = normalize(tokens)
    hot_rows = row_steps(own_ids, step_of_sample, step_count)
    shifts, scales = modulation(hot_rows, step_table)
    modded = (normed * (1.0 + scales) + shifts).astype(jnp.bfloat16)
    grad_block = grad_q
    partial_grad = lax.dot_general(
        lax.all_gather(modded, "tensor", axis=0, tiled=True),
        grad_block,
        (((0,), (0,)), ((), ())),
        preferred_element_type=jnp.float32,
    )
    grad_weight = lax.psum_scatter(
        partial_grad.astype(jnp.bfloat16), "dp", scatter_dimension=0, tiled=True
    ).astype(jnp.float32)
    grad_block = grad_q
    grad_mod = lax.psum_scatter(
        lax.dot_general(
            grad_block, weight, (((1,), (1,)), ((), ())), preferred_element_type=jnp.float32
        ).astype(jnp.bfloat16),
        "tensor",
        scatter_dimension=0,
        tiled=True,
    ).astype(jnp.float32)
    grad_normed = grad_mod * (1.0 + scales)
    mean_grad = jnp.mean(grad_normed, axis=-1, keepdims=True)
    mean_proj = jnp.mean(grad_normed * normed, axis=-1, keepdims=True)
    grad_x = ((grad_normed - mean_grad - normed * mean_proj) * inv_std).astype(jnp.bfloat16)
    shift_sum = jnp.dot(hot_rows.T, grad_mod, precision=lax.Precision.HIGHEST)
    scale_sum = jnp.dot(hot_rows.T, grad_mod * normed, precision=lax.Precision.HIGHEST)
    local_sums = jnp.stack([shift_sum, scale_sum], axis=1)
    grad_table = lax.psum(local_sums, ("tensor", "dp"))
    return (grad_x, grad_weight, grad_table)


def solution(mesh):
    placed = (
        P(("dp", "tensor"), None),
        P("dp", None),
        P("dp", None),
        P(),
        P(None, "tensor"),
        P("dp", "tensor"),
    )
    return jax.shard_map(
        body,
        mesh=mesh,
        in_specs=placed,
        out_specs=(P(("dp", "tensor"), None), P("dp", "tensor"), P()),
        check_vma=False,
    )
```

profile of v0, /device:TPU:19, one launch (start us, length us, event | category | flops | bytes accessed | tf_op | source)
XLA Modules:
  0.0 671.1 jit_solution(6565208928526798029)
XLA Ops:
  7.2 0.0 copy-start
  7.2 0.0 reduce-scatter.3.cloned.1.call-start
  7.2 1.1 copy-done
  8.3 11.9 %convolution_convert_fusion = bf16[1024,6144]{1,0:T(8,128)(2,1)} fusion(bf16[1024,384]{1,0:T(8,128)(2,1)S(1)} %copy-done, bf16[6144,384]{1,0:T(8,128)(2,1)} %param.10), kind=kOutput, calls=%fused_computation | convolution fusion | flops 4838129664 | bytes 18087936 | tf_op jit(solution)/shard_map/dot_general | solution.py:56
  20.2 0.0 reduce-scatter.3.cloned.1.call-update
  20.3 0.0 copy-start.4
  20.3 0.0 copy-start.2
  20.3 0.0 all-gather.2.cloned.1.call-start
  20.3 3.6 copy.11
  23.9 0.0 copy-start.3
  23.9 0.8 dynamic-slice_bitcast_fusion
  24.7 0.0 copy-done.4
  24.7 0.1 select_reduce_fusion
  24.8 0.0 copy-done.2
  24.8 0.3 convert_reduce_fusion
  25.1 0.6 fusion.11
  25.7 0.0 copy-done.3
  25.7 4.6 fusion.15
  30.2 67.0 %reduce-scatter.3.cloned.1.call-done = bf16[128,6144]{1,0:T(8,128)(2,1)} async-done(((bf16[1024,6144]{1,0:T(8,128)(2,1)}), bf16[128,6144]{1,0:T(8,128)(2,1)}) %reduce-scatter.3.cloned.1.call-update) | async-done | bytes 1572880 | tf_op jit(solution)/shard_map/reduce_scatter | solution.py:55
  97.2 0.0 copy-start.1
  97.2 3.5 fusion.14
  100.8 0.7 copy-done.1
  101.4 3.7 fusion.10
  105.2 0.0 all-gather.2.cloned.1.call-update
  105.2 0.0 all-reduce.2.cloned.1.call-start
  105.3 1.9 convolution_bitcast_fusion.1
  107.1 3.2 convolution_bitcast_fusion
  110.3 1.3 pad_maximum_fusion
  111.6 0.0 all-reduce.2.cloned.1.call-update
  111.6 0.2 reduce-scatter.5.cloned.1.call-start
  111.9 63.7 %all-gather.2.cloned.1.call-done = bf16[1024,6144]{1,0:T(8,128)(2,1)} async-done(((bf16[128,6144]{1,0:T(8,128)(2,1)}), bf16[1024,6144]{1,0:T(8,128)(2,1)}) %all-gather.2.cloned.1.call-update) | async-done | bytes 12582928 | tf_op jit(solution)/shard_map/all_gather | solution.py:46
  175.6 11.1 %convolution_convert_fusion.1 = bf16[6144,384]{1,0:T(8,128)(2,1)} fusion(bf16[1024,6144]{1,0:T(8,128)(2,1)} %all-gather.2.cloned.1.call-done, bf16[1024,384]{1,0:T(8,128)(2,1)S(1)} %copy-done), kind=kOutput, calls=%fused_computation.1 | convolution fusion | flops 4834197504 | bytes 18087936 | tf_op jit(solution)/shard_map/dot_general | solution.py:45
  186.7 0.0 reduce-scatter.5.cloned.1.call-update
  186.7 252.4 %all-reduce.2.cloned.1.call-done = f32[32,2,6144]{2,0,1:T(8,128)} async-done(((f32[32,2,6144]{2,0,1:T(8,128)}), f32[32,2,6144]{2,0,1:T(8,128)}) %all-reduce.2.cloned.1.call-update) | async-done | bytes 1572880 | tf_op jit(solution)/shard_map/psum | solution.py:70
  439.2 3.8 copy.10
  442.9 220.0 %reduce-scatter.5.cloned.1.call-done = bf16[192,384]{1,0:T(8,128)(2,1)} async-done(((bf16[6144,384]{1,0:T(8,128)(2,1)}), bf16[192,384]{1,0:T(8,128)(2,1)}) %reduce-scatter.5.cloned.1.call-update) | async-done | bytes 147472 | tf_op jit(solution)/shard_map/reduce_scatter | solution.py:51
  662.9 1.6 convert_element_type.29
  (3 shorter events, 0.0 us)
Async XLA Ops:
  7.2 1.1 copy-start
  7.2 90.1 %reduce-scatter.3.cloned.1.call-start = ((), (), s32[]{:S(2)}) async-start(), calls=%async_computation.2 | async-start | bytes 14155776 | tf_op jit(solution)/shard_map/reduce_scatter | solution.py:55
  20.3 4.4 copy-start.4
  20.3 4.5 copy-start.2
  20.3 155.3 %all-gather.2.cloned.1.call-start = ((), (), s32[]{:S(2)}) async-start(), calls=%async_computation.3 | async-start | bytes 14155776 | tf_op jit(solution)/shard_map/all_gather | solution.py:46
  23.9 1.7 copy-start.3
  97.2 4.2 copy-start.1
  105.2 333.9 %all-reduce.2.cloned.1.call-start = ((), (), s32[]{:S(2)}) async-start(), calls=%async_computation.5 | async-start | bytes 3145728 | tf_op jit(solution)/shard_map/psum | solution.py:70
  111.6 551.3 %reduce-scatter.5.cloned.1.call-start = ((), (), s32[]{:S(2)}) async-start(), calls=%async_computation.4 | async-start | bytes 4866048 | tf_op jit(solution)/shard_map/reduce_scatter | solution.py:51
Sparse Core Ops, SparseCore 0:
  20.4 76.8 reduce-scatter.2
  105.3 70.1 all-gather.1
  180.9 258.1 all-reduce.1
  443.5 219.4 reduce-scatter.4
where the time goes:
time: 677 us; the launch traced here: 671 us
  waiting for transfers between devices  603 us (89%)
  matrix products  32.7 us (5%)
  between operations  13.8 us (2%)
  other arithmetic  11.2 us (2%)
  local copies, waits for them, and re-layouts  9.87 us (1%)
    psum x1, waiting for transfers between devices, body(): grad_table = lax.psum(local_sums, ('tensor', 'dp'))  252 us
    reduce_scatter x1, waiting for transfers between devices, body(): lax.psum_scatter(partial_grad.astype(jnp.bfloat16), 'dp', scatter_dimensi...  220 us
    reduce_scatter x1, waiting for transfers between devices, body(): lax.psum_scatter(lax.dot_general(grad_block, weight, (((1,), (1,)), ((),...  67 us
    all_gather x1, waiting for transfers between devices, body(): lax.all_gather(modded, 'tensor', axis=0, tiled=True)  63.7 us
  transfers between devices with their start and end apart: 4, of which 4 were waited for; matrix products, arithmetic and copies ran while one was open for 5% of the time, Pallas kernels for 0%

commit v1 on v0

v1 whole, which is shorter than its diff:
```python
import jax
import jax.numpy as jnp
from jax import lax
from jax.experimental import pallas as pl
from jax.experimental.pallas import tpu as pltpu
from jax.sharding import PartitionSpec as P

MESH = pl.DeviceIdType.MESH
F32 = jnp.float32
BF16 = jnp.bfloat16

D = 6144
TOK = 128
ROWS = 1024
STEPS = 32
GW = 384
DS = 768
NT = 8
NDP = 32
WZ = 32
WY = 128
WYO = 256
PR = 96
ROUND = (0, 1, 3, 2)


def rem(a, b):
    return lax.rem(a, jnp.int32(b))


def div(a, b):
    return lax.div(a, jnp.int32(b))


def kernel(
    tok_h, sid_ref, ts_ref, tab_h, w_h, gq_h,
    gx_h, gw_h, gt_h,
    tok, nrm32, nrm16, inv, scl, tab, tab_d, hot3, nd, modt, gq, w, part, rs_r, rs_l, fin_s, fin,
    gmacc, gms, gmr, gxv, gwv, tsum, trecv, ttot, tfull,
    loc, ws, wr, ags, agr, ys, yr, ns, nr, qs, qr, rss, rsr, fs, fr, gs, gr, tse, tre, xs, xr_sem,
):
    t = lax.axis_index("tensor")
    p = lax.axis_index("dp")
    x, c = div(t, 2), rem(t, 2)
    y, z = div(p, 8), rem(p, 8)

    def at(tt, pp):
        return {"tensor": tt, "dp": pp}

    def xc(dx, cc):
        return rem(x + dx, 4) * 2 + cc

    def zy(dy, dz):
        return rem(y + dy, 4) * 8 + rem(z + dz, 8)

    sent = []

    def remote(src, dst, s, r, dev, start=True):
        cp = pltpu.make_async_remote_copy(
            src_ref=src, dst_ref=dst, send_sem=s, recv_sem=r, device_id=dev, device_id_type=MESH
        )
        if start:
            cp.start()
            sent.append(cp)
        return cp

    def arrived(dst, s, r):
        pltpu.make_async_remote_copy(
            src_ref=dst, dst_ref=dst, send_sem=s, recv_sem=r, device_id=at(t, p), device_id_type=MESH
        ).wait_recv()

    bar = pltpu.get_barrier_semaphore()
    for i in range(1, NT):
        pl.semaphore_signal(bar, inc=1, device_id=at(rem(t + i, NT), p), device_id_type=MESH)

    def greet(i, _):
        pl.semaphore_signal(bar, inc=1, device_id=at(t, rem(p + i, NDP)), device_id_type=MESH)
        return 0

    lax.fori_loop(1, NDP, greet, 0)
    for yy in range(4):
        for h in range(2):
            pl.semaphore_signal(
                bar, inc=1, device_id=at(div(p, 4), yy * 8 + 2 * rem(p, 4) + h), device_id_type=MESH
            )

    def cols(cc):
        return pl.ds(pl.multiple_of(cc * GW, GW), GW)

    def slice_cols(tt):
        return pl.ds(pl.multiple_of(tt * DS, DS), DS)

    cp_tok = pltpu.make_async_copy(tok_h, tok, loc.at[0])
    cp_tok.start()
    cp_tab = pltpu.make_async_copy(tab_h, tab, loc.at[1])
    cp_tab.start()
    cp_td = pltpu.make_async_copy(tab_h.at[:, :, slice_cols(t)], tab_d, loc.at[2])
    cp_td.start()
    cp_gq = pltpu.make_async_copy(gq_h, gq.at[x, :, cols(c)], loc.at[3])
    cp_gq.start()
    cp_wz = pltpu.make_async_copy(
        w_h.at[pl.ds(t * DS + z * WZ, WZ), :], w.at[x, pl.ds(z * WZ, WZ), cols(c)], loc.at[4]
    )
    cp_wz.start()
    cp_wy = pltpu.make_async_copy(
        w_h.at[pl.ds(t * DS + WYO + y * WY, WY), :], w.at[x, pl.ds(WYO + y * WY, WY), cols(c)], loc.at[5]
    )
    cp_wy.start()

    pl.semaphore_wait(bar, NT - 1 + NDP - 1 + 8)

    for i in range(1, NT):
        tt = rem(t + i, NT)
        remote(
            w_h.at[pl.ds(tt * DS + z * WZ, WZ), :], w.at[x, pl.ds(z * WZ, WZ), cols(c)],
            ws.at[0, i], wr.at[0, i], at(tt, p),
        )
        remote(
            w_h.at[pl.ds(tt * DS + WYO + y * WY, WY), :], w.at[x, pl.ds(WYO + y * WY, WY), cols(c)],
            ws.at[1, i], wr.at[1, i], at(tt, p),
        )

    cp_tok.wait()

    def norm(i, _):
        rows = pl.ds(i * 16, 16)
        v = tok[rows, :].astype(F32)
        v = v - jnp.mean(v, axis=-1, keepdims=True)
        k = lax.rsqrt(jnp.mean(v * v, axis=-1, keepdims=True) + 1e-06)
        v = v * k
        nrm32[rows, :] = v
        inv[rows, :] = jnp.broadcast_to(k, (16, 128))
        for j in range(NT):
            nrm16[j, rows, :] = v[:, j * DS : (j + 1) * DS].astype(BF16)
        return 0

    lax.fori_loop(0, TOK // 16, norm, 0)
    for i in (4, 5, 2, 3, 6, 7, 1):
        tt = rem(t + i, NT)
        remote(nrm16.at[tt], nd.at[t], ns.at[i], nr.at[i], at(tt, p))
    nd[t] = nrm16[t]

    def half(h):
        return pl.ds(h * 512, 512)

    right, left, sib = at(xc(1, c), p), at(xc(3, c), p), at(xc(0, 1 - c), p)
    remote(gq_h.at[half(0), :], gq.at[x, half(0), cols(c)], qs.at[0], qr.at[0], right)
    remote(gq_h.at[half(1), :], gq.at[x, half(1), cols(c)], qs.at[1], qr.at[1], left)
    remote(gq_h.at[half(1), :], gq.at[x, half(1), cols(c)], qs.at[2], qr.at[2], right)
    remote(gq_h.at[half(0), :], gq.at[x, half(0), cols(c)], qs.at[3], qr.at[3], left)
    remote(gq_h, gq.at[x, :, cols(c)], qs.at[4], qr.at[4], sib)

    step = jnp.zeros((1, ROWS), jnp.int32)
    for s in range(8):
        step = step + jnp.where(sid_ref[...] == s, ts_ref[0:1, s : s + 1], 0)
    hot = (lax.broadcasted_iota(jnp.int32, (STEPS, ROWS), 0) == step).astype(F32).astype(BF16)
    for k in range(3):
        hot3[k * STEPS : (k + 1) * STEPS, :] = hot

    def thirds(v):
        hi = v.astype(BF16)
        rest = v - hi.astype(F32)
        mid = rest.astype(BF16)
        lo = (rest - mid.astype(F32)).astype(BF16)
        return jnp.concatenate([hi, mid, lo], axis=0)

    def pick(h, table):
        return lax.dot_general(h, thirds(table), (((0,), (0,)), ((), ())), preferred_element_type=F32)

    cp_tab.wait()
    own = hot3[:, pl.ds(pl.multiple_of(t * TOK, TOK), TOK)]
    for j in range(NT):
        js = slice(j * DS, (j + 1) * DS)
        scl[:, js] = pick(own, 1.0 + tab[:, 1, js])

    cp_wz.wait()
    for i in range(1, NT):
        s = rem(t + NT - i, NT)
        arrived(w.at[div(s, 2), pl.ds(z * WZ, WZ), cols(rem(s, 2))], ws.at[0, i], wr.at[0, i])

    def wz(d, k=None):
        r = pl.ds(rem(z + d + 8, 8) * WZ, WZ)
        return w.at[:, r, :] if k is None else w.at[pl.ds(2 * k, 2), r, :]

    def gather_z(s):
        a, b = (wz(-s), wz(s)) if s < 3 else (wz(-s, 0), wz(s, 1))
        remote(a, a, ags.at[0, s], agr.at[0, s], at(t, zy(0, 1)))
        remote(b, b, ags.at[1, s], agr.at[1, s], at(t, zy(0, 7)))

    def gathered_z(s):
        a, b = (wz(-1 - s), wz(1 + s)) if s < 3 else (wz(-1 - s, 0), wz(1 + s, 1))
        arrived(a, ags.at[0, s], agr.at[0, s])
        arrived(b, ags.at[1, s], agr.at[1, s])

    def wy(d):
        return w.at[:, pl.ds(WYO + rem(y + d, 4) * WY, WY), :]

    gather_z(0)
    cp_wy.wait()
    for i in range(1, NT):
        s = rem(t + NT - i, NT)
        arrived(w.at[div(s, 2), pl.ds(WYO + y * WY, WY), cols(rem(s, 2))], ws.at[1, i], wr.at[1, i])
    for i in (1, 3, 2):
        remote(wy(0), wy(0), ys.at[i], yr.at[i], at(t, zy(i, 0)))
    for s in range(3):
        gathered_z(s)
        gather_z(s + 1)

    for i in range(1, NT):
        arrived(nd.at[rem(t + NT - i, NT)], ns.at[i], nr.at[i])
    cp_td.wait()
    shift3 = thirds(tab_d[:, 0, :])
    scale3 = thirds(1.0 + tab_d[:, 1, :])

    for i in range(4):
        h = hot3[:, i * 256 : (i + 1) * 256]
        sh = lax.dot_general(h, shift3, (((0,), (0,)), ((), ())), preferred_element_type=F32)
        sc = lax.dot_general(h, scale3, (((0,), (0,)), ((), ())), preferred_element_type=F32)
        m = nd[2 * i : 2 * i + 2].reshape(256, DS).astype(F32) * sc + sh
        modt[:, i * 256 : (i + 1) * 256] = m.T.astype(BF16)

    def partial(r):
        xx = rem(x + ROUND[r], 4)

        def rowblock(i, _):
            rows = pl.ds(pl.multiple_of(i * 256, 256), 256)
            part[r, rows, :] = jnp.dot(modt[rows, :], gq[xx], preferred_element_type=F32).astype(BF16)
            return 0

        lax.fori_loop(0, 3, rowblock, 0)

    A, B = slice(0, GW), slice(GW, DS)

    def piece(d):
        return pl.ds(pl.multiple_of(rem(z + d + 8, 8) * PR, PR), PR)

    def rs_send(r, s):
        if s == 0:
            a = (part.at[r, piece(4), A], rs_r.at[r, s, :, A])
            b = (part.at[r, piece(4), B], rs_l.at[r, s, :, B])
        else:
            a = (part.at[r, piece(4 - s), :], rs_r.at[r, s])
            b = (part.at[r, piece(s - 4), :], rs_l.at[r, s])
        remote(*a, rss.at[0, r, s], rsr.at[0, r, s], at(t, zy(0, 1)))
        remote(*b, rss.at[1, r, s], rsr.at[1, r, s], at(t, zy(0, 7)))

    def add(r, pc, cc, got):
        part[r, pc, cc] = (part[r, pc, cc].astype(F32) + got.astype(F32)).astype(BF16)

    def rs_step(r, s):
        if s == 0:
            arrived(rs_r.at[r, s, :, A], rss.at[0, r, s], rsr.at[0, r, s])
            add(r, piece(3), A, rs_r[r, s, :, A])
            arrived(rs_l.at[r, s, :, B], rss.at[1, r, s], rsr.at[1, r, s])
            add(r, piece(-3), B, rs_l[r, s, :, B])
        elif s < 3:
            arrived(rs_r.at[r, s], rss.at[0, r, s], rsr.at[0, r, s])
            add(r, piece(3 - s), slice(None), rs_r[r, s])
            arrived(rs_l.at[r, s], rss.at[1, r, s], rsr.at[1, r, s])
            add(r, piece(s - 3), slice(None), rs_l[r, s])
        if s < 3:
            rs_send(r, s + 1)
            return
        arrived(rs_r.at[r, s], rss.at[0, r, s], rsr.at[0, r, s])
        arrived(rs_l.at[r, s], rss.at[1, r, s], rsr.at[1, r, s])
        v = part[r, piece(0), :].astype(F32) + rs_r[r, s].astype(F32) + rs_l[r, s].astype(F32)
        xx = rem(x + ROUND[r], 4)
        pp = 4 * t + div(z, 2)
        for k in range(2):
            fin_s[r, k] = v[:, k * GW : (k + 1) * GW].astype(BF16)
            dst, rs = fin.at[y, rem(z, 2)], fr.at[y, rem(z, 2)]
            if r > 0:
                remote(fin_s.at[r, k], dst, fs.at[r, k], rs, at(2 * xx + k, pp))
            else:
                me = jnp.logical_and(pp == p, c == k)

                @pl.when(me)
                def _():
                    pltpu.make_async_copy(fin_s.at[r, k], dst, rs).start()

                @pl.when(jnp.logical_not(me))
                def _():
                    remote(fin_s.at[r, k], dst, fs.at[r, k], rs, at(2 * xx + k, pp))
                    sent.pop()

    def gm_add(xx, first):
        def rowblock(i, _):
            rows = pl.ds(pl.multiple_of(i * 256, 256), 256)
            v = lax.dot_general(gq[xx, rows, :], w[xx], (((1,), (1,)), ((), ())), preferred_element_type=F32)
            gmacc[rows, :] = v if first else gmacc[rows, :] + v
            return 0

        lax.fori_loop(0, 4, rowblock, 0)

    def forward(xx, hh, k):
        v = gq.at[xx, hh, cols(c)]
        remote(v, v, qs.at[k], qr.at[k], sib)

    def got(xx, hh, cc, k):
        arrived(gq.at[xx, hh, cols(cc)], qs.at[k], qr.at[k])

    x1, x2, x3 = rem(x + 1, 4), rem(x + 2, 4), rem(x + 3, 4)
    full = pl.ds(0, ROWS)
    cp_gq.wait()
    got(x, full, 1 - c, 4)
    partial(0)
    rs_send(0, 0)
    gathered_z(3)
    for i in (1, 3, 2):
        arrived(wy(4 - i), ys.at[i], yr.at[i])
    rs_step(0, 0)
    gm_add(x, True)
    rs_step(0, 1)
    rs_step(0, 2)
    got(x3, half(0), c, 0)
    remote(gq.at[x3, half(0), cols(c)], gq.at[x3, half(0), cols(c)], qs.at[5], qr.at[5], right)
    forward(x3, half(0), 7)
    got(x1, half(1), c, 1)
    remote(gq.at[x1, half(1), cols(c)], gq.at[x1, half(1), cols(c)], qs.at[6], qr.at[6], left)
    forward(x1, half(1), 8)
    rs_step(0, 3)
    got(x3, half(1), c, 2)
    forward(x3, half(1), 9)
    got(x1, half(0), c, 3)
    forward(x1, half(0), 10)
    got(x1, half(1), 1 - c, 8)
    got(x1, half(0), 1 - c, 10)
    partial(1)
    rs_send(1, 0)
    got(x3, half(0), 1 - c, 7)
    got(x3, half(1), 1 - c, 9)
    partial(2)
    rs_send(2, 0)
    rs_step(1, 0)
    rs_step(2, 0)
    gm_add(x1, False)
    rs_step(1, 1)
    gm_add(x3, False)
    rs_step(2, 1)
    got(x2, half(0), c, 5)
    forward(x2, half(0), 11)
    got(x2, half(1), c, 6)
    forward(x2, half(1), 12)
    rs_step(1, 2)
    got(x2, half(0), 1 - c, 11)
    got(x2, half(1), 1 - c, 12)

    for k in (2, 1, 3, 0):
        xx = rem(x + k, 4)
        rows = pl.ds(pl.multiple_of(xx * 256, 256), 256)
        v = lax.dot_general(gq[x2, rows, :], w[x2], (((1,), (1,)), ((), ())), preferred_element_type=F32)
        v = gmacc[rows, :] + v
        gms[pl.ds(2 * xx, 2)] = v.astype(BF16).reshape(2, TOK, DS)
        for cc in range(2):
            tt = 2 * xx + (c if cc == 0 else 1 - c)
            if k == 0 and cc == 0:
                gmr[t] = gms[t]
            else:
                remote(gms.at[tt], gmr.at[t], gs.at[k, cc], gr.at[k, cc], at(tt, p))
    partial(3)
    rs_send(3, 0)
    rs_step(2, 2)
    rs_step(1, 3)

    hot1 = hot3[0:STEPS, :]
    gmv = gms[...].reshape(ROWS, DS)
    tsum[:, 0, :] = jnp.dot(hot1, gmv, preferred_element_type=F32)
    prod = (gmv.astype(F32) * nd[...].reshape(ROWS, DS).astype(F32)).astype(BF16)
    tsum[:, 1, :] = jnp.dot(hot1, prod, preferred_element_type=F32)
    cp_t0 = pltpu.make_async_copy(tsum.at[p], trecv.at[p], tre.at[0])
    cp_t0.start()

    def scatter(i, _):
        q = rem(p + i, NDP)
        pltpu.make_async_remote_copy(
            src_ref=tsum.at[q], dst_ref=trecv.at[p], send_sem=tse.at[0], recv_sem=tre.at[0],
            device_id=at(t, q), device_id_type=MESH,
        ).start()
        return 0

    lax.fori_loop(1, NDP, scatter, 0)
    rs_step(3, 0)
    rs_step(2, 3)
    rs_step(3, 1)
    pltpu.make_async_copy(trecv, trecv, tre.at[0]).wait()
    ttot[...] = jnp.sum(trecv[...], axis=0)
    cp_t1 = pltpu.make_async_copy(ttot, tfull.at[p], tre.at[1])
    cp_t1.start()

    def spread(i, _):
        q = rem(p + i, NDP)
        pltpu.make_async_remote_copy(
            src_ref=ttot, dst_ref=tfull.at[p], send_sem=tse.at[1], recv_sem=tre.at[1],
            device_id=at(t, q), device_id_type=MESH,
        ).start()
        return 0

    lax.fori_loop(1, NDP, spread, 0)
    rs_step(3, 2)
    rs_step(3, 3)
    pltpu.make_async_copy(tfull, tfull, tre.at[1]).wait()

    def gt(tt):
        return gt_h.at[:, :, slice_cols(tt)]

    cp_gt = pltpu.make_async_copy(tfull, gt(t), loc.at[6])
    cp_gt.start()
    for k in (2, 1, 3):
        remote(tfull, gt(t), xs.at[k], xr_sem.at[k], at(xc(k, c), p))
    remote(tfull, gt(t), xs.at[0], xr_sem.at[0], sib)

    for k in (1, 3, 2, 0):
        for cc in range(2):
            if k == 0 and cc == 0:
                continue
            arrived(gmr.at[2 * rem(x + 4 - k, 4) + (c if cc == 0 else 1 - c)], gs.at[k, cc], gr.at[k, cc])

    def back(i, _):
        rows = pl.ds(i * 16, 16)
        gn = [gmr[j, rows, :].astype(F32) * scl[rows, j * DS : (j + 1) * DS] for j in range(NT)]
        nv = [nrm32[rows, j * DS : (j + 1) * DS] for j in range(NT)]
        m1 = sum(jnp.sum(g, axis=-1, keepdims=True) for g in gn) * (1.0 / D)
        m2 = sum(jnp.sum(g * n, axis=-1, keepdims=True) for g, n in zip(gn, nv)) * (1.0 / D)
        k = inv[rows, 0:1]
        for j in range(NT):
            gxv[rows, j * DS : (j + 1) * DS] = ((gn[j] - m1 - nv[j] * m2) * k).astype(BF16)
        return 0

    lax.fori_loop(0, TOK // 16, back, 0)
    cp_gx = pltpu.make_async_copy(gxv, gx_h, loc.at[7])
    cp_gx.start()

    for k in (1, 3, 2):
        s = xc(4 - k, c)
        arrived(gt(s), xs.at[k], xr_sem.at[k])
        remote(gt(s), gt(s), xs.at[3 + k], xr_sem.at[3 + k], sib)

    for h in range(2):
        for yy in range(4):
            arrived(fin.at[yy, h], fs.at[0, 0], fr.at[yy, h])
        gwv[h * PR : (h + 1) * PR, :] = sum(fin[yy, h].astype(F32) for yy in range(4))
    cp_gw = pltpu.make_async_copy(gwv, gw_h, loc.at[8])
    cp_gw.start()

    arrived(gt(xc(0, 1 - c)), xs.at[0], xr_sem.at[0])
    for k in (1, 3, 2):
        s = xc(4 - k, 1 - c)
        arrived(gt(s), xs.at[3 + k], xr_sem.at[3 + k])
    cp_gt.wait()
    cp_gx.wait()
    cp_gw.wait()
    for cp in sent:
        cp.wait_send()
    for k in range(2):
        me = jnp.logical_and(4 * t + div(z, 2) == p, c == k)

        @pl.when(jnp.logical_not(me))
        def _():
            remote(fin_s.at[0, k], fin.at[y, rem(z, 2)], fs.at[0, k], fr.at[y, rem(z, 2)], at(2 * x + k, p), start=False).wait_send()

    pltpu.make_async_copy(trecv.at[pl.ds(0, NDP - 1)], trecv.at[pl.ds(0, NDP - 1)], tse.at[0]).wait()
    pltpu.make_async_copy(trecv.at[pl.ds(0, NDP - 1)], trecv.at[pl.ds(0, NDP - 1)], tse.at[1]).wait()


def body(tokens, sample_id, timestep, step_table, weight, grad_q):
    any_spec = pl.BlockSpec(memory_space=pl.ANY)
    vmem_spec = pl.BlockSpec(memory_space=pltpu.VMEM)
    dma = pltpu.SemaphoreType.DMA
    return pl.pallas_call(
        kernel,
        name="fused_backward",
        out_shape=(
            jax.ShapeDtypeStruct((TOK, D), BF16),
            jax.ShapeDtypeStruct((2 * PR, GW), F32),
            jax.ShapeDtypeStruct((STEPS, 2, D), F32),
        ),
        in_specs=[any_spec, vmem_spec, vmem_spec, any_spec, any_spec, any_spec],
        out_specs=(any_spec, any_spec, any_spec),
        scratch_shapes=[
            pltpu.VMEM((TOK, D), BF16),
            pltpu.VMEM((TOK, D), F32),
            pltpu.VMEM((NT, TOK, DS), BF16),
            pltpu.VMEM((TOK, 128), F32),
            pltpu.VMEM((TOK, D), F32),
            pltpu.VMEM((STEPS, 2, D), F32),
            pltpu.VMEM((STEPS, 2, DS), F32),
            pltpu.VMEM((3 * STEPS, ROWS), BF16),
            pltpu.VMEM((NT, TOK, DS), BF16),
            pltpu.VMEM((DS, ROWS), BF16),
            pltpu.VMEM((4, ROWS, DS), BF16),
            pltpu.VMEM((4, DS, DS), BF16),
            pltpu.VMEM((4, DS, DS), BF16),
            pltpu.VMEM((4, 4, PR, DS), BF16),
            pltpu.VMEM((4, 4, PR, DS), BF16),
            pltpu.VMEM((4, 2, PR, GW), BF16),
            pltpu.VMEM((4, 2, PR, GW), BF16),
            pltpu.VMEM((ROWS, DS), F32),
            pltpu.VMEM((NT, TOK, DS), BF16),
            pltpu.VMEM((NT, TOK, DS), BF16),
            pltpu.VMEM((TOK, D), BF16),
            pltpu.VMEM((2 * PR, GW), F32),
            pltpu.VMEM((STEPS, 2, DS), F32),
            pltpu.VMEM((NDP, 2, DS), F32),
            pltpu.VMEM((2, DS), F32),
            pltpu.VMEM((STEPS, 2, DS), F32),
            dma((9,)),
            dma((2, NT)), dma((2, NT)),
            dma((2, 4)), dma((2, 4)),
            dma((4,)), dma((4,)),
            dma((NT,)), dma((NT,)),
            dma((13,)), dma((13,)),
            dma((2, 4, 4)), dma((2, 4, 4)),
            dma((4, 2)), dma((4, 2)),
            dma((4, 2)), dma((4, 2)),
            dma((2,)), dma((2,)),
            dma((7,)), dma((7,)),
        ],
        cost_estimate=pl.CostEstimate(flops=9_700_000_000, bytes_accessed=14_000_000, transcendentals=0),
        compiler_params=pltpu.CompilerParams(
            collective_id=0, has_side_effects=True, vmem_limit_bytes=60 * 2**20
        ),
    )(tokens, sample_id, timestep, step_table, weight, grad_q)


def solution(mesh):
    placed = (
        P(("dp", "tensor"), None),
        P("dp", None),
        P("dp", None),
        P(),
        P(None, "tensor"),
        P("dp", "tensor"),
    )
    return jax.shard_map(
        body,
        mesh=mesh,
        in_specs=placed,
        out_specs=(P(("dp", "tensor"), None), P("dp", "tensor"), P()),
        check_vma=False,
    )
```

time: 677 us -> 162 us (0.24)
  waiting for transfers between devices: 603 us -> 0 us
  Pallas kernels: 0 us -> 154 us
  matrix products: 32.7 us -> 0 us
  between operations: 13.8 us -> 0.66 us
  other arithmetic: 11.2 us -> 0 us
    reduce_scatter x2 -> x0, waiting for transfers between devices: 287 us -> none  [the longest x1 220 us: body(): lax.psum_scatter(partial_grad.astype(jnp.bfloat16), 'dp', scatter_dimensi...]
    psum x1 -> x0, waiting for transfers between devices: 252 us -> none  [body(): grad_table = lax.psum(local_sums, ('tensor', 'dp'))]
    pallas_call x0 -> x1, Pallas kernels: none -> 154 us  [body(): pl.pallas_call(kernel, name='fused_backward', out_shape=(jax.ShapeDtypeSt...]
    all_gather x1 -> x0, waiting for transfers between devices: 63.7 us -> none  [body(): lax.all_gather(modded, 'tensor', axis=0, tiled=True)]
    dot_general x5 -> x0, matrix products: 32.7 us -> none  [the longest x1 11.9 us: body(): lax.dot_general(grad_block, weight, (((1,), (1,)), ((), ())), preferred_e...]
  transfers between devices with their start and end apart: 4 -> 0, of which waited for: 4 -> 0; matrix products, arithmetic and copies ran while one was open for 5% -> 0% of each run, Pallas kernels for 0% -> 0%
where the time goes in v1:
time: 162 us; the launch traced here: 159 us
  Pallas kernels  154 us (95%)
  local copies, waits for them, and re-layouts  4.69 us (3%)
    pallas_call x1, Pallas kernels, body(): pl.pallas_call(kernel, name='fused_backward', out_shape=(jax.ShapeDtypeSt...  154 us
    unnamed x7, local copies, waits for them, and re-layouts  4.69 us

profile of v1, /device:TPU:19, one launch (start us, length us, event | category | flops | bytes accessed | tf_op | source)
XLA Modules:
  0.0 159.5 jit_solution(12759161713450687224)
XLA Ops:
  0.6 154.1 %fused_backward.1 = (bf16[128,6144]{1,0:T(8,128)(2,1)}, f32[192,384]{1,0:T(8,128)}, f32[32,2,6144]{2,1,0:T(2,128)}) custom-call(bf16[128,6144]{1,0:T(8,128)(2,1)} %tok_h.1, s32[1,1024]{1,0:T(1,128)} %sid_ref.1, s32[1,8]{1,0:T(1,128)} %ts_ref.1, f32[32,2,6144]{2,1,0:T(2,128)} %tab_h.1, bf16[6144,384]{1,0:T(8,128)(2,1)} %w_h.1, bf16[1024,384]{1,0:T(8,128)(2,1)} %gq_h.1), custom_call_target="tpu_custom_call" | custom-call | flops 9699999744 | bytes 14000000 | tf_op jit(solution)/shard_map/fused_backward/pallas_call | solution.py:469
  154.8 0.0 copy-start.1
  154.8 0.0 copy-start
  154.8 2.8 %copy.12 = bf16[128,6144]{1,0:T(8,128)(2,1)} copy(bf16[128,6144]{1,0:T(8,128)(2,1)} %get-tuple-element.6) | data formatting | bytes 3145728
  157.6 0.0 copy-done.1
  157.6 0.7 copy.13
  158.3 0.0 copy-done
  158.3 1.1 copy.14
Async XLA Ops:
  154.8 2.8 %copy-start.1 = (f32[192,384]{1,0:T(8,128)S(1)}, f32[192,384]{1,0:T(8,128)}, u32[]{:S(2)}) copy-start(f32[192,384]{1,0:T(8,128)} %get-tuple-element.7) | copy-start | bytes 884740
  154.8 3.6 %copy-start = (f32[32,2,6144]{2,1,0:T(2,128)S(1)}, f32[32,2,6144]{2,1,0:T(2,128)}, u32[]{:S(2)}) copy-start(f32[32,2,6144]{2,1,0:T(2,128)} %get-tuple-element.8) | copy-start | bytes 4718596

commit v2 on v1

v2 whole, which is shorter than its diff:
```python
import jax
import jax.numpy as jnp
from jax import lax
from jax.experimental import pallas as pl
from jax.experimental.pallas import tpu as pltpu
from jax.sharding import PartitionSpec as P

MESH = pl.DeviceIdType.MESH
F32 = jnp.float32
BF16 = jnp.bfloat16

D = 6144
TOK = 128
ROWS = 1024
STEPS = 32
GW = 384
DS = 768
NT = 8
NDP = 32
WZ = 64
WY = 64
WYO = 512
PY = 192
PZ = 48
ROUND = (0, 1, 3, 2)


def rem(a, b):
    return lax.rem(a, jnp.int32(b))


def div(a, b):
    return lax.div(a, jnp.int32(b))


def kernel(
    tok_h, sid_ref, ts_ref, tab_h, w_h, gq_h,
    gx_h, gw_h, gt_h,
    tok, nrm32, nrm16, inv, scl, tab, tab_d, hot3, nd, modt, gq, w, part, y0, y1, zs, zr, fin, gwr, gwv,
    gmacc, gms, gmr, gxv, tsum, tz, tp, ty, tt_v, tfull, tb,
    loc, ws, wr, ags, agr, ys, yr, ns, nr, qs, qr, rss, rsr, zss, zsr, fs, fr, gs, gr, tse, tre, tys, tyr, xs, xr_sem,
):
    t = lax.axis_index("tensor")
    p = lax.axis_index("dp")
    x, c = div(t, 2), rem(t, 2)
    y, z = div(p, 8), rem(p, 8)

    def at(tt, pp):
        return {"tensor": tt, "dp": pp}

    def xc(dx, cc):
        return rem(x + dx, 4) * 2 + cc

    def zy(dy, dz):
        return rem(y + dy, 4) * 8 + rem(z + dz, 8)

    sent = []

    def remote(src, dst, s, r, dev, start=True):
        cp = pltpu.make_async_remote_copy(
            src_ref=src, dst_ref=dst, send_sem=s, recv_sem=r, device_id=dev, device_id_type=MESH
        )
        if start:
            cp.start()
            sent.append(cp)
        return cp

    def arrived(dst, s, r):
        pltpu.make_async_remote_copy(
            src_ref=dst, dst_ref=dst, send_sem=s, recv_sem=r, device_id=at(t, p), device_id_type=MESH
        ).wait_recv()

    bar = pltpu.get_barrier_semaphore()
    for i in range(1, NT):
        pl.semaphore_signal(bar, inc=1, device_id=at(rem(t + i, NT), p), device_id_type=MESH)

    for i in range(1, 8):
        pl.semaphore_signal(bar, inc=1, device_id=at(t, zy(0, i)), device_id_type=MESH)
    for i in range(1, 4):
        pl.semaphore_signal(bar, inc=1, device_id=at(t, zy(i, 0)), device_id_type=MESH)
    for q in range(4):
        pl.semaphore_signal(
            bar, inc=1, device_id=at(div(p, 4), rem(p, 4) * 8 + 2 * q + c), device_id_type=MESH
        )

    def cols(cc):
        return pl.ds(pl.multiple_of(cc * GW, GW), GW)

    def slice_cols(tt):
        return pl.ds(pl.multiple_of(tt * DS, DS), DS)

    cp_tok = pltpu.make_async_copy(tok_h, tok, loc.at[0])
    cp_tok.start()
    cp_tab = pltpu.make_async_copy(tab_h, tab, loc.at[1])
    cp_tab.start()
    cp_td = pltpu.make_async_copy(tab_h.at[:, :, slice_cols(t)], tab_d, loc.at[2])
    cp_td.start()
    cp_gq = pltpu.make_async_copy(gq_h, gq.at[x, :, cols(c)], loc.at[3])
    cp_gq.start()
    cp_wz = pltpu.make_async_copy(
        w_h.at[pl.ds(t * DS + z * WZ, WZ), :], w.at[x, pl.ds(z * WZ, WZ), cols(c)], loc.at[4]
    )
    cp_wz.start()
    cp_wy = pltpu.make_async_copy(
        w_h.at[pl.ds(t * DS + WYO + y * WY, WY), :], w.at[x, pl.ds(WYO + y * WY, WY), cols(c)], loc.at[5]
    )
    cp_wy.start()

    pl.semaphore_wait(bar, NT - 1 + 7 + 3 + 4)

    for i in range(1, NT):
        tt = rem(t + i, NT)
        remote(
            w_h.at[pl.ds(tt * DS + z * WZ, WZ), :], w.at[x, pl.ds(z * WZ, WZ), cols(c)],
            ws.at[0, i], wr.at[0, i], at(tt, p),
        )
        remote(
            w_h.at[pl.ds(tt * DS + WYO + y * WY, WY), :], w.at[x, pl.ds(WYO + y * WY, WY), cols(c)],
            ws.at[1, i], wr.at[1, i], at(tt, p),
        )

    cp_tok.wait()

    def norm(i, _):
        rows = pl.ds(i * 16, 16)
        v = tok[rows, :].astype(F32)
        v = v - jnp.mean(v, axis=-1, keepdims=True)
        k = lax.rsqrt(jnp.mean(v * v, axis=-1, keepdims=True) + 1e-06)
        v = v * k
        nrm32[rows, :] = v
        inv[rows, :] = jnp.broadcast_to(k, (16, 128))
        for j in range(NT):
            nrm16[j, rows, :] = v[:, j * DS : (j + 1) * DS].astype(BF16)
        return 0

    lax.fori_loop(0, TOK // 16, norm, 0)
    for i in (4, 5, 2, 3, 6, 7, 1):
        tt = rem(t + i, NT)
        remote(nrm16.at[tt], nd.at[t], ns.at[i], nr.at[i], at(tt, p))
    nd[t] = nrm16[t]

    def half(h):
        return pl.ds(h * 512, 512)

    right, left, sib = at(xc(1, c), p), at(xc(3, c), p), at(xc(0, 1 - c), p)

    step = jnp.zeros((1, ROWS), jnp.int32)
    for s in range(8):
        step = step + jnp.where(sid_ref[...] == s, ts_ref[0:1, s : s + 1], 0)
    level = lax.broadcasted_iota(jnp.int32, (2 * STEPS, ROWS), 0)
    hot_shift = (level == 2 * step).astype(F32).astype(BF16)
    hot_scale = (level == 2 * step + 1).astype(F32).astype(BF16)
    hot = (lax.broadcasted_iota(jnp.int32, (STEPS, ROWS), 0) == step).astype(F32).astype(BF16)
    for k in range(3):
        hot3[k * STEPS : (k + 1) * STEPS, :] = hot

    def thirds(v):
        hi = v.astype(BF16)
        rest = v - hi.astype(F32)
        mid = rest.astype(BF16)
        lo = (rest - mid.astype(F32)).astype(BF16)
        return jnp.concatenate([hi, mid, lo], axis=0)

    def pick(h, table):
        return lax.dot_general(h, thirds(table), (((0,), (0,)), ((), ())), preferred_element_type=F32)

    cp_tab.wait()
    own = hot3[:, pl.ds(pl.multiple_of(t * TOK, TOK), TOK)]
    for j in range(NT):
        js = slice(j * DS, (j + 1) * DS)
        scl[:, js] = pick(own, 1.0 + tab[:, 1, js])

    def forward(xx, hh, k):
        v = gq.at[xx, hh, cols(c)]
        remote(v, v, qs.at[k], qr.at[k], sib)

    def got(xx, hh, cc, k):
        arrived(gq.at[xx, hh, cols(cc)], qs.at[k], qr.at[k])

    x1, x2, x3 = rem(x + 1, 4), rem(x + 2, 4), rem(x + 3, 4)

    def arrived_rows(which):
        for i in which:
            arrived(nd.at[rem(t + NT - i, NT)], ns.at[i], nr.at[i])

    cp_wz.wait()
    for i in range(1, NT):
        s = rem(t + NT - i, NT)
        arrived(w.at[div(s, 2), pl.ds(z * WZ, WZ), cols(rem(s, 2))], ws.at[0, i], wr.at[0, i])

    def wz(d, k=None):
        r = pl.ds(rem(z + d + 8, 8) * WZ, WZ)
        return w.at[:, r, :] if k is None else w.at[pl.ds(2 * k, 2), r, :]

    def gather_z(s):
        a, b = (wz(-s), wz(s)) if s < 3 else (wz(-s, 0), wz(s, 1))
        remote(a, a, ags.at[0, s], agr.at[0, s], at(t, zy(0, 1)))
        remote(b, b, ags.at[1, s], agr.at[1, s], at(t, zy(0, 7)))

    def gathered_z(s):
        a, b = (wz(-1 - s), wz(1 + s)) if s < 3 else (wz(-1 - s, 0), wz(1 + s, 1))
        arrived(a, ags.at[0, s], agr.at[0, s])
        arrived(b, ags.at[1, s], agr.at[1, s])

    def wy(d):
        return w.at[:, pl.ds(WYO + rem(y + d, 4) * WY, WY), :]

    gather_z(0)
    cp_wy.wait()
    for i in range(1, NT):
        s = rem(t + NT - i, NT)
        arrived(w.at[div(s, 2), pl.ds(WYO + y * WY, WY), cols(rem(s, 2))], ws.at[1, i], wr.at[1, i])
    for i in (1, 3, 2):
        remote(wy(0), wy(0), ys.at[i], yr.at[i], at(t, zy(i, 0)))
    arrived_rows((2, 6))
    remote(gq_h.at[half(0), :], gq.at[x, half(0), cols(c)], qs.at[0], qr.at[0], right)
    remote(gq_h.at[half(1), :], gq.at[x, half(1), cols(c)], qs.at[1], qr.at[1], left)
    remote(gq_h.at[half(1), :], gq.at[x, half(1), cols(c)], qs.at[2], qr.at[2], right)
    remote(gq_h.at[half(0), :], gq.at[x, half(0), cols(c)], qs.at[3], qr.at[3], left)
    remote(gq_h, gq.at[x, :, cols(c)], qs.at[4], qr.at[4], sib)
    gathered_z(0)
    gather_z(1)

    arrived_rows((1, 3, 4, 5, 7))
    cp_td.wait()
    shift3 = thirds(tab_d[:, 0, :])
    scale3 = thirds(1.0 + tab_d[:, 1, :])

    for i in range(4):
        h = hot3[:, i * 256 : (i + 1) * 256]
        sh = lax.dot_general(h, shift3, (((0,), (0,)), ((), ())), preferred_element_type=F32)
        sc = lax.dot_general(h, scale3, (((0,), (0,)), ((), ())), preferred_element_type=F32)
        m = nd[2 * i : 2 * i + 2].reshape(256, DS).astype(F32) * sc + sh
        modt[:, i * 256 : (i + 1) * 256] = m.T.astype(BF16)

    def partial(r):
        xx = rem(x + ROUND[r], 4)

        def rowblock(i, _):
            rows = pl.ds(pl.multiple_of(i * 256, 256), 256)
            part[r, rows, :] = jnp.dot(modt[rows, :], gq[xx], preferred_element_type=F32).astype(BF16)
            return 0

        lax.fori_loop(0, 3, rowblock, 0)

    A, B = slice(0, GW), slice(GW, DS)
    up, down = at(t, zy(1, 0)), at(t, zy(3, 0))

    def piece(d):
        return pl.ds(pl.multiple_of(rem(y + d, 4) * PY, PY), PY)

    def y_send(r):
        for k, (d, cc, dst, dev) in enumerate(
            ((2, A, y0.at[0, r], up), (1, B, y1.at[0, r, :, B], up))
        ):
            remote(part.at[r, piece(d), cc], dst, rss.at[0, r, k], rsr.at[0, r, k], dev)
        for k, (d, cc, dst, dev) in enumerate(
            ((2, B, y0.at[1, r], down), (3, A, y1.at[1, r, :, A], down))
        ):
            remote(part.at[r, piece(d), cc], dst, rss.at[1, r, k], rsr.at[1, r, k], dev)

    def y_pass(r):
        for k, (d, cc, dev) in enumerate(((1, A, up), (3, B, down))):
            arrived(y0.at[k, r], rss.at[k, r, 0], rsr.at[k, r, 0])
            v = part[r, piece(d), cc].astype(F32) + y0[k, r].astype(F32)
            part[r, piece(d), cc] = v.astype(BF16)
            remote(part.at[r, piece(d), cc], y1.at[k, r, :, cc], rss.at[k, r, 2], rsr.at[k, r, 2], dev)

    def z_send(r):
        for k, (early, late) in enumerate(((B, A), (A, B))):
            arrived(y1.at[k, r, :, early], rss.at[k, r, 1], rsr.at[k, r, 1])
            arrived(y1.at[k, r, :, late], rss.at[k, r, 2], rsr.at[k, r, 2])
        v = part[r, piece(0), :].astype(F32) + y1[0, r].astype(F32) + y1[1, r].astype(F32)
        for k in range(8):
            rows, cc = slice((k // 2) * PZ, (k // 2 + 1) * PZ), (A, B)[k % 2]
            zs[r, k] = v[rows, cc].astype(BF16)
        pltpu.make_async_copy(zs.at[r, z], zr.at[r, z], zsr.at[r]).start()

        def spread_z(i, _):
            zz = rem(z + i, 8)
            pltpu.make_async_remote_copy(
                src_ref=zs.at[r, zz], dst_ref=zr.at[r, z], send_sem=zss.at[r], recv_sem=zsr.at[r],
                device_id=at(t, y * 8 + zz), device_id_type=MESH,
            ).start()
            return 0

        lax.fori_loop(1, 8, spread_z, 0)

    def owner(r, start):
        xx = rem(x + ROUND[r], 4)
        tt, pp = 2 * xx + rem(z, 2), 4 * t + y
        q = div(z, 2)
        dst = gwr.at[q]
        cp = remote(fin.at[r], dst, fs.at[r], fr.at[q], at(tt, pp), start=False)
        if r > 0:
            if start:
                cp.start()
            else:
                cp.wait_send()
            return
        me = jnp.logical_and(tt == t, pp == p)

        @pl.when(me)
        def _():
            if start:
                pltpu.make_async_copy(fin.at[r], dst, fr.at[q]).start()

        @pl.when(jnp.logical_not(me))
        def _():
            if start:
                cp.start()
            else:
                cp.wait_send()

    def z_sum(r):
        pltpu.make_async_copy(zr.at[r], zr.at[r], zsr.at[r]).wait()
        fin[r] = jnp.sum(zr[r].astype(F32), axis=0).astype(BF16)
        owner(r, True)

    def gm_add(xx, first):
        def rowblock(i, _):
            rows = pl.ds(pl.multiple_of(i * 256, 256), 256)
            v = lax.dot_general(gq[xx, rows, :], w[xx], (((1,), (1,)), ((), ())), preferred_element_type=F32)
            gmacc[rows, :] = v if first else gmacc[rows, :] + v
            return 0

        lax.fori_loop(0, 4, rowblock, 0)

    full = pl.ds(0, ROWS)
    cp_gq.wait()
    got(x, full, 1 - c, 4)
    partial(0)
    y_send(0)
    gathered_z(1)
    gather_z(2)
    y_pass(0)
    gathered_z(2)
    gather_z(3)
    got(x3, half(0), c, 0)
    remote(gq.at[x3, half(0), cols(c)], gq.at[x3, half(0), cols(c)], qs.at[5], qr.at[5], right)
    forward(x3, half(0), 7)
    got(x1, half(1), c, 1)
    remote(gq.at[x1, half(1), cols(c)], gq.at[x1, half(1), cols(c)], qs.at[6], qr.at[6], left)
    forward(x1, half(1), 8)
    got(x3, half(1), c, 2)
    forward(x3, half(1), 9)
    got(x1, half(0), c, 3)
    forward(x1, half(0), 10)
    z_send(0)
    got(x1, half(1), 1 - c, 8)
    got(x1, half(0), 1 - c, 10)
    partial(1)
    y_send(1)
    got(x3, half(0), 1 - c, 7)
    got(x3, half(1), 1 - c, 9)
    partial(2)
    y_send(2)
    gathered_z(3)
    for i in (1, 3, 2):
        arrived(wy(4 - i), ys.at[i], yr.at[i])
    gm_add(x, True)
    got(x2, half(0), c, 5)
    forward(x2, half(0), 11)
    got(x2, half(1), c, 6)
    forward(x2, half(1), 12)
    gm_add(x1, False)
    y_pass(1)
    got(x2, half(0), 1 - c, 11)
    got(x2, half(1), 1 - c, 12)
    partial(3)
    y_send(3)
    gm_add(x3, False)

    for k in (2, 1, 3, 0):
        xx = rem(x + k, 4)
        rows = pl.ds(pl.multiple_of(xx * 256, 256), 256)
        v = lax.dot_general(gq[x2, rows, :], w[x2], (((1,), (1,)), ((), ())), preferred_element_type=F32)
        v = gmacc[rows, :] + v
        gms[pl.ds(2 * xx, 2)] = v.astype(BF16).reshape(2, TOK, DS)
        for cc in range(2):
            tt = 2 * xx + (c if cc == 0 else 1 - c)
            if k == 0 and cc == 0:
                gmr[t] = gms[t]
            else:
                remote(gms.at[tt], gmr.at[t], gs.at[k, cc], gr.at[k, cc], at(tt, p))
    def spread_table(src, dst, k):
        pltpu.make_async_copy(src(z), dst.at[z], tre.at[k]).start()
        for i in range(1, 8):
            zz = rem(z + i, 8)
            pltpu.make_async_remote_copy(
                src_ref=src(zz), dst_ref=dst.at[z], send_sem=tse.at[k], recv_sem=tre.at[k],
                device_id=at(t, y * 8 + zz), device_id_type=MESH,
            ).start()

    y_pass(2)
    z_send(1)
    y_pass(3)
    gmv = gms[...].reshape(ROWS, DS)
    prod = (gmv.astype(F32) * nd[...].reshape(ROWS, DS).astype(F32)).astype(BF16)
    sums = jnp.dot(hot_shift, gmv, preferred_element_type=F32) + jnp.dot(hot_scale, prod, preferred_element_type=F32)
    tsum[...] = sums.reshape(8, 8, DS)
    spread_table(lambda zz: tsum.at[zz], tz, 0)
    z_send(2)
    z_send(3)
    z_sum(0)
    pltpu.make_async_copy(tz, tz, tre.at[0]).wait()
    tp[...] = jnp.sum(tz[...], axis=0)
    ty[y] = tp[...]
    for i in (1, 3, 2):
        remote(tp, ty.at[y], tys.at[i], tyr.at[i], at(t, zy(i, 0)))
    z_sum(1)
    z_sum(2)
    for i in (1, 3, 2):
        arrived(ty.at[rem(y + 4 - i, 4)], tys.at[i], tyr.at[i])
    tt_v[...] = ty[0] + ty[1] + ty[2] + ty[3]
    spread_table(lambda zz: tt_v, tfull, 1)
    z_sum(3)
    pltpu.make_async_copy(tfull, tfull, tre.at[1]).wait()
    tb[...] = tfull[...].reshape(2 * STEPS, DS).astype(BF16)

    def gt(tt):
        return gt_h.at[:, slice_cols(tt)]

    cp_gt = pltpu.make_async_copy(tb, gt(t), loc.at[6])
    cp_gt.start()
    for k in (2, 1, 3):
        remote(tb, gt(t), xs.at[k], xr_sem.at[k], at(xc(k, c), p))
    remote(tb, gt(t), xs.at[0], xr_sem.at[0], sib)

    for k in (1, 3, 2, 0):
        for cc in range(2):
            if k == 0 and cc == 0:
                continue
            arrived(gmr.at[2 * rem(x + 4 - k, 4) + (c if cc == 0 else 1 - c)], gs.at[k, cc], gr.at[k, cc])

    def back(i, _):
        rows = pl.ds(i * 16, 16)
        gn = [gmr[j, rows, :].astype(F32) * scl[rows, j * DS : (j + 1) * DS] for j in range(NT)]
        nv = [nrm32[rows, j * DS : (j + 1) * DS] for j in range(NT)]
        m1 = sum(jnp.sum(g, axis=-1, keepdims=True) for g in gn) * (1.0 / D)
        m2 = sum(jnp.sum(g * n, axis=-1, keepdims=True) for g, n in zip(gn, nv)) * (1.0 / D)
        k = inv[rows, 0:1]
        for j in range(NT):
            gxv[rows, j * DS : (j + 1) * DS] = ((gn[j] - m1 - nv[j] * m2) * k).astype(BF16)
        return 0

    lax.fori_loop(0, TOK // 16, back, 0)
    cp_gx = pltpu.make_async_copy(gxv, gx_h, loc.at[7])
    cp_gx.start()

    for k in (1, 3, 2):
        s = xc(4 - k, c)
        arrived(gt(s), xs.at[k], xr_sem.at[k])
        remote(gt(s), gt(s), xs.at[3 + k], xr_sem.at[3 + k], sib)

    for q in range(4):
        arrived(gwr.at[q], fs.at[0], fr.at[q])
    gwv[...] = gwr[...].astype(F32).reshape(PY, GW)
    cp_gw = pltpu.make_async_copy(gwv, gw_h, loc.at[8])
    cp_gw.start()
    arrived(gt(xc(0, 1 - c)), xs.at[0], xr_sem.at[0])
    for k in (1, 3, 2):
        s = xc(4 - k, 1 - c)
        arrived(gt(s), xs.at[3 + k], xr_sem.at[3 + k])
    cp_gt.wait()
    cp_gx.wait()
    cp_gw.wait()
    for cp in sent:
        cp.wait_send()
    for r in range(4):
        owner(r, False)
        pltpu.make_async_copy(zr.at[r, pl.ds(0, 7)], zr.at[r, pl.ds(0, 7)], zss.at[r]).wait()
    for k in range(2):
        pltpu.make_async_copy(tz.at[pl.ds(0, 7)], tz.at[pl.ds(0, 7)], tse.at[k]).wait()


def body(tokens, sample_id, timestep, step_table, weight, grad_q):
    any_spec = pl.BlockSpec(memory_space=pl.ANY)
    vmem_spec = pl.BlockSpec(memory_space=pltpu.VMEM)
    dma = pltpu.SemaphoreType.DMA
    grad_x, grad_weight, table = pl.pallas_call(
        kernel,
        name="fused_backward",
        out_shape=(
            jax.ShapeDtypeStruct((TOK, D), BF16),
            jax.ShapeDtypeStruct((PY, GW), F32),
            jax.ShapeDtypeStruct((2 * STEPS, D), BF16),
        ),
        in_specs=[any_spec, vmem_spec, vmem_spec, any_spec, any_spec, any_spec],
        out_specs=(any_spec, any_spec, any_spec),
        scratch_shapes=[
            pltpu.VMEM((TOK, D), BF16),
            pltpu.VMEM((TOK, D), F32),
            pltpu.VMEM((NT, TOK, DS), BF16),
            pltpu.VMEM((TOK, 128), F32),
            pltpu.VMEM((TOK, D), F32),
            pltpu.VMEM((STEPS, 2, D), F32),
            pltpu.VMEM((STEPS, 2, DS), F32),
            pltpu.VMEM((3 * STEPS, ROWS), BF16),
            pltpu.VMEM((NT, TOK, DS), BF16),
            pltpu.VMEM((DS, ROWS), BF16),
            pltpu.VMEM((4, ROWS, DS), BF16),
            pltpu.VMEM((4, DS, DS), BF16),
            pltpu.VMEM((4, DS, DS), BF16),
            pltpu.VMEM((2, 4, PY, GW), BF16),
            pltpu.VMEM((2, 4, PY, DS), BF16),
            pltpu.VMEM((4, 8, PZ, GW), BF16),
            pltpu.VMEM((4, 8, PZ, GW), BF16),
            pltpu.VMEM((4, PZ, GW), BF16),
            pltpu.VMEM((4, PZ, GW), BF16),
            pltpu.VMEM((PY, GW), F32),
            pltpu.VMEM((ROWS, DS), F32),
            pltpu.VMEM((NT, TOK, DS), BF16),
            pltpu.VMEM((NT, TOK, DS), BF16),
            pltpu.VMEM((TOK, D), BF16),
            pltpu.VMEM((8, 8, DS), F32),
            pltpu.VMEM((8, 8, DS), F32),
            pltpu.VMEM((8, DS), F32),
            pltpu.VMEM((4, 8, DS), F32),
            pltpu.VMEM((8, DS), F32),
            pltpu.VMEM((8, 8, DS), F32),
            pltpu.VMEM((2 * STEPS, DS), BF16),
            dma((9,)),
            dma((2, NT)), dma((2, NT)),
            dma((2, 4)), dma((2, 4)),
            dma((4,)), dma((4,)),
            dma((NT,)), dma((NT,)),
            dma((13,)), dma((13,)),
            dma((2, 4, 3)), dma((2, 4, 3)),
            dma((4,)), dma((4,)),
            dma((4,)), dma((4,)),
            dma((4, 2)), dma((4, 2)),
            dma((2,)), dma((2,)),
            dma((4,)), dma((4,)),
            dma((7,)), dma((7,)),
        ],
        cost_estimate=pl.CostEstimate(flops=9_700_000_000, bytes_accessed=14_000_000, transcendentals=0),
        compiler_params=pltpu.CompilerParams(
            collective_id=0, has_side_effects=True, vmem_limit_bytes=60 * 2**20
        ),
    )(tokens, sample_id, timestep, step_table, weight, grad_q)
    return (grad_x, grad_weight, table.astype(F32).reshape(STEPS, 2, D))


def solution(mesh):
    placed = (
        P(("dp", "tensor"), None),
        P("dp", None),
        P("dp", None),
        P(),
        P(None, "tensor"),
        P("dp", "tensor"),
    )
    return jax.shard_map(
        body,
        mesh=mesh,
        in_specs=placed,
        out_specs=(P(("dp", "tensor"), None), P("dp", "tensor"), P()),
        check_vma=False,
    )
```

time: 162 us -> 129 us (0.80); the launches traced: 159 us -> 129 us
  Pallas kernels: 154 us -> 123 us
    pallas_call x1, Pallas kernels: 154 us -> 123 us  [body(): pl.pallas_call(kernel, name='fused_backward', out_shape=(jax.ShapeDtypeSt...]
    reshape x0 -> x1, local copies, waits for them, and re-layouts: none -> 3.12 us  [body(): return (grad_x, grad_weight, table.astype(F32).reshape(STEPS, 2, D))]
    unnamed x7 -> x6, local copies, waits for them, and re-layouts: 4.69 us -> 1.86 us
where the time goes in v2:
time: 129 us
  Pallas kernels  123 us (95%)
  local copies, waits for them, and re-layouts  4.99 us (4%)
    pallas_call x1, Pallas kernels, body(): pl.pallas_call(kernel, name='fused_backward', out_shape=(jax.ShapeDtypeSt...  123 us
    reshape x1, local copies, waits for them, and re-layouts, body(): return (grad_x, grad_weight, table.astype(F32).reshape(STEPS, 2, D))  3.12 us

profile of v2, /device:TPU:19, one launch (start us, length us, event | category | flops | bytes accessed | tf_op | source)
XLA Modules:
  0.0 128.6 jit_solution(15865687398167867376)
XLA Ops:
  0.6 122.9 %fused_backward.1 = (bf16[128,6144]{1,0:T(8,128)(2,1)}, f32[192,384]{1,0:T(8,128)}, bf16[64,6144]{1,0:T(8,128)(2,1)}) custom-call(bf16[128,6144]{1,0:T(8,128)(2,1)} %tok_h.1, s32[1,1024]{1,0:T(1,128)} %sid_ref.1, s32[1,8]{1,0:T(1,128)} %ts_ref.1, f32[32,2,6144]{2,1,0:T(2,128)} %tab_h.1, bf16[6144,384]{1,0:T(8,128)(2,1)} %w_h.1, bf16[1024,384]{1,0:T(8,128)(2,1)} %gq_h.1), custom_call_target="tpu_custom_call" | custom-call | flops 9699999744 | bytes 14000000 | tf_op jit(solution)/shard_map/fused_backward/pallas_call | solution.py:481
  123.6 0.0 copy-start
  123.6 3.1 %reshape.15 = f32[32,2,6144]{2,1,0:T(2,128)} reshape(bf16[64,6144]{1,0:T(8,128)(2,1)} %get-tuple-element.8) | data formatting | bytes 2359296 | tf_op jit(solution)/shard_map/reshape | solution.py:542
  126.7 0.0 copy-done
  126.7 0.0 copy-start.1
  126.7 1.1 copy.11
  127.9 0.0 copy-done.1
  127.9 0.7 copy.12
Async XLA Ops:
  123.6 3.1 %copy-start = (bf16[128,6144]{1,0:T(8,128)(2,1)S(1)}, bf16[128,6144]{1,0:T(8,128)(2,1)}, u32[]{:S(2)}) copy-start(bf16[128,6144]{1,0:T(8,128)(2,1)} %get-tuple-element.12) | copy-start | bytes 4718596
  126.7 1.1 copy-start.1

commit v3 on v2

--- a/solution.py
+++ b/solution.py
@@ -367,8 +367,6 @@
     y_pass(1)
     got(x2, half(0), 1 - c, 11)
     got(x2, half(1), 1 - c, 12)
-    partial(3)
-    y_send(3)
     gm_add(x3, False)
 
     for k in (2, 1, 3, 0):
@@ -392,29 +390,29 @@
                 device_id=at(t, y * 8 + zz), device_id_type=MESH,
             ).start()
 
-    y_pass(2)
-    z_send(1)
-    y_pass(3)
     gmv = gms[...].reshape(ROWS, DS)
     prod = (gmv.astype(F32) * nd[...].reshape(ROWS, DS).astype(F32)).astype(BF16)
     sums = jnp.dot(hot_shift, gmv, preferred_element_type=F32) + jnp.dot(hot_scale, prod, preferred_element_type=F32)
     tsum[...] = sums.reshape(8, 8, DS)
     spread_table(lambda zz: tsum.at[zz], tz, 0)
-    z_send(2)
-    z_send(3)
-    z_sum(0)
+    partial(3)
+    y_send(3)
+    y_pass(2)
+    z_send(1)
     pltpu.make_async_copy(tz, tz, tre.at[0]).wait()
     tp[...] = jnp.sum(tz[...], axis=0)
     ty[y] = tp[...]
     for i in (1, 3, 2):
         remote(tp, ty.at[y], tys.at[i], tyr.at[i], at(t, zy(i, 0)))
-    z_sum(1)
-    z_sum(2)
+    y_pass(3)
+    z_send(2)
     for i in (1, 3, 2):
         arrived(ty.at[rem(y + 4 - i, 4)], tys.at[i], tyr.at[i])
     tt_v[...] = ty[0] + ty[1] + ty[2] + ty[3]
     spread_table(lambda zz: tt_v, tfull, 1)
-    z_sum(3)
+    z_sum(0)
+    z_send(3)
+    z_sum(1)
     pltpu.make_async_copy(tfull, tfull, tre.at[1]).wait()
     tb[...] = tfull[...].reshape(2 * STEPS, DS).astype(BF16)
 
@@ -426,6 +424,12 @@
     for k in (2, 1, 3):
         remote(tb, gt(t), xs.at[k], xr_sem.at[k], at(xc(k, c), p))
     remote(tb, gt(t), xs.at[0], xr_sem.at[0], sib)
+    z_sum(2)
+    z_sum(3)
+    for k in (1, 3, 2):
+        u = xc(4 - k, c)
+        arrived(gt(u), xs.at[k], xr_sem.at[k])
+        remote(gt(u), gt(u), xs.at[3 + k], xr_sem.at[3 + k], sib)
 
     for k in (1, 3, 2, 0):
         for cc in range(2):
@@ -447,11 +451,6 @@
     lax.fori_loop(0, TOK // 16, back, 0)
     cp_gx = pltpu.make_async_copy(gxv, gx_h, loc.at[7])
     cp_gx.start()
-
-    for k in (1, 3, 2):
-        s = xc(4 - k, c)
-        arrived(gt(s), xs.at[k], xr_sem.at[k])
-        remote(gt(s), gt(s), xs.at[3 + k], xr_sem.at[3 + k], sib)
 
     for q in range(4):
         arrived(gwr.at[q], fs.at[0], fr.at[q])

time: 129 us -> 127 us (0.984)
  the two profiles are of different devices: /device:TPU:19 before, /device:TPU:16 now
where the time goes in v3:
time: 127 us; the launch traced here: 126 us
  Pallas kernels  121 us (95%)
  local copies, waits for them, and re-layouts  4.99 us (4%)
    pallas_call x1, Pallas kernels, body(): pl.pallas_call(kernel, name='fused_backward', out_shape=(jax.ShapeDtypeSt...  121 us
    reshape x1, local copies, waits for them, and re-layouts, body(): return (grad_x, grad_weight, table.astype(F32).reshape(STEPS, 2, D))  3.12 us

profile of v3, /device:TPU:16, one launch (start us, length us, event | category | flops | bytes accessed | tf_op | source)
XLA Modules:
  0.0 126.4 jit_solution(2085942172943409095)
XLA Ops:
  0.6 120.7 %fused_backward.1 = (bf16[128,6144]{1,0:T(8,128)(2,1)}, f32[192,384]{1,0:T(8,128)}, bf16[64,6144]{1,0:T(8,128)(2,1)}) custom-call(bf16[128,6144]{1,0:T(8,128)(2,1)} %tok_h.1, s32[1,1024]{1,0:T(1,128)} %sid_ref.1, s32[1,8]{1,0:T(1,128)} %ts_ref.1, f32[32,2,6144]{2,1,0:T(2,128)} %tab_h.1, bf16[6144,384]{1,0:T(8,128)(2,1)} %w_h.1, bf16[1024,384]{1,0:T(8,128)(2,1)} %gq_h.1), custom_call_target="tpu_custom_call" | custom-call | flops 9699999744 | bytes 14000000 | tf_op jit(solution)/shard_map/fused_backward/pallas_call | solution.py:480
  121.4 0.0 copy-start
  121.4 3.1 %reshape.15 = f32[32,2,6144]{2,1,0:T(2,128)} reshape(bf16[64,6144]{1,0:T(8,128)(2,1)} %get-tuple-element.8) | data formatting | bytes 2359296 | tf_op jit(solution)/shard_map/reshape | solution.py:541
  124.5 0.0 copy-done
  124.5 0.0 copy-start.1
  124.5 1.1 copy.11
  125.7 0.0 copy-done.1
  125.7 0.7 copy.12
Async XLA Ops:
  121.4 3.1 %copy-start = (bf16[128,6144]{1,0:T(8,128)(2,1)S(1)}, bf16[128,6144]{1,0:T(8,128)(2,1)}, u32[]{:S(2)}) copy-start(bf16[128,6144]{1,0:T(8,128)(2,1)} %get-tuple-element.12) | copy-start | bytes 4718596
  124.5 1.1 copy-start.1
